TPU v7x, 128 devices: a whole 4x4x4 slice. The times are simulated.
128 devices in a mesh: col: 8 (over x_hi, y), row: 16 (over z, x_lo, core).
Axes of the slice: x: 4 (x_hi: 2, x_lo: 2; x = x_hi * 2 + x_lo), y: 4, z: 4, core: 2. Of those that a mesh axis runs over, the one named last changes fastest.
Arguments:
- corner_top_left: bfloat16 [800, 1600], P('col', 'row'), may hold values from -0.625 to 0.625
- corner_top_right: bfloat16 [800, 1600], P('col', 'row'), may hold values from -0.625 to 0.625
- corner_bottom_left: bfloat16 [800, 1600], P('col', 'row'), may hold values from -0.625 to 0.625
- edge_top: bfloat16 [800, 40000], P('col', 'row'), may hold values from -6 to 6
- edge_right: bfloat16 [800, 40000], P('col', 'row'), may hold values from -6 to 6
- edge_bottom: bfloat16 [800, 40000], P('col', 'row'), may hold values from -6 to 6
- edge_left: bfloat16 [800, 40000], P('col', 'row'), may hold values from -6 to 6
- tensors: bfloat16 [8, 625, 625], replicated, may hold values from -0.25 to 0.25
- pattern: int32 [8, 16], P('col', 'row'), may hold values from 0 to 7, as said below
- sketch_below: float32 [100, 100], replicated, may hold values from -0.4375 to 0.4375
- sketch_above: float32 [100, 100], replicated, may hold values from -0.4375 to 0.4375
- sketch_right: float32 [100, 100], replicated, may hold values from -0.4375 to 0.4375
- sketch_left: float32 [100, 100], replicated, may hold values from -0.4375 to 0.4375
Outputs:
- left_corner_top: bfloat16 [800, 1600], P('col', 'row')
- left_edge: bfloat16 [800, 40000], P('col', 'row')
- left_corner_bottom: bfloat16 [800, 1600], P('col', 'row')
- top_corner_left: bfloat16 [800, 1600], P('col', 'row')
- top_edge: bfloat16 [800, 40000], P('col', 'row')
- top_corner_right: bfloat16 [800, 1600], P('col', 'row')
Inputs may be any that keep to these rules, and one draw needn't show every extreme that they name: `pattern`: each of the 8 tensors sits at exactly 16 sites.
All inputs are finite; a program needn't handle non-finite values.
Results may differ from a plain program's by a relative error of at most 0.039.
Values may be sent and summed in bfloat16 or wider, within the bound.
A program may use at most 192 MiB of HBM per device.

v0:
```python
import functools

import jax
import jax.numpy as jnp
from jax import lax
from jax.experimental import pallas as pl
from jax.experimental.pallas import tpu as pltpu
from jax.sharding import PartitionSpec as P

CHI = 100
DD = 25
LANE = 128
ROWS = 112
MAIN = DD - 1
WIDE = DD * LANE
SQUARE = 640
DEPTH = 2560
PAIRS = 13
GROUP = 20
BATCH = 2
BF = jnp.bfloat16
F32 = jnp.float32
MESH = pl.DeviceIdType.MESH


def dot(a, b):
    return jnp.dot(a, b, preferred_element_type=F32)


def dot_exact(a, b):
    return lax.dot_general(
        a, b, (((1,), (0,)), ((), ())), precision=lax.Precision.HIGHEST,
        preferred_element_type=F32,
    )


def split(values):
    high = values.astype(BF)
    return high, (values - high.astype(F32)).astype(BF)


def block(k):
    return slice(LANE * k, LANE * (k + 1))


def widen(source, target):
    target[...] = jnp.zeros_like(target)
    for k in range(DD):
        target[0:CHI, LANE * k : LANE * k + CHI] = source[:, CHI * k : CHI * (k + 1)]


def pad_square(source, target):
    target[...] = jnp.zeros_like(target)
    target[0:CHI, 0:CHI] = source[...]


def rms(values):
    scale = jnp.sqrt(jnp.sum(values * values) / (CHI * CHI) + 1e-06)
    return values / scale


def factor_inverse(gram, work):
    rows = lax.broadcasted_iota(jnp.int32, (LANE, LANE), 0)
    columns = lax.broadcasted_iota(jnp.int32, (LANE, LANE), 1)
    eye = (rows == columns).astype(F32)
    work[:, 0:LANE] = gram
    work[:, LANE:] = eye
    inner = lax.broadcasted_iota(jnp.int32, (8, LANE), 0)
    for start in range(0, 104, 8):
        halves = [work[start : start + 8, block(n)] for n in range(2)]
        tall = [
            jnp.broadcast_to(halves[0][:, start + n : start + n + 1], (8, LANE)) for n in range(8)
        ]
        for step in range(8):
            if start + step >= CHI:
                break
            inverse = lax.rsqrt(jnp.broadcast_to(tall[step][step : step + 1], (8, LANE)))
            factor = tall[step] * inverse
            for later in range(step + 1, 8):
                tall[later] = tall[later] - factor * factor[later : later + 1]
            for n in range(2):
                row = halves[n][step : step + 1] * inverse
                halves[n] = jnp.where(
                    inner < step,
                    halves[n],
                    jnp.where(inner == step, row, halves[n] - factor * row),
                )
        panel = jnp.concatenate(halves, axis=1)
        work[start : start + 8, :] = panel
        if start + 8 < 104:
            high = panel.astype(BF).astype(F32)
            middle = (panel - high).astype(BF).astype(F32)
            low = panel - high - middle
            tall_parts = [part[:, :LANE] for part in (high, high, high, middle, middle, low)]
            update = lax.dot_general(
                jnp.concatenate(tall_parts, axis=0).T.astype(BF),
                jnp.concatenate([high, middle, low, high, middle, high], axis=0).astype(BF),
                (((1,), (0,)), ((), ())), preferred_element_type=F32,
            )
            work[start + 8 : 104, :] = work[start + 8 : 104, :] - update[start + 8 : 104, :]
    inverse = work[:, LANE:]
    return jnp.where((rows >= CHI) & (rows != columns), 0.0, inverse)


def frame_of(sketched, others, cholesky, wide_frame, by_row, turned):
    count = len(others) + 1
    total = jnp.zeros((LANE, count * LANE), F32)
    for k in range(DD):
        own = sketched[:, block(k)]
        right = jnp.concatenate([own] + [other[:, block(k)] for other in others], axis=1)
        total = total + lax.dot_general(
            own, right, (((0,), (0,)), ((), ())), preferred_element_type=F32
        )
    rows = lax.broadcasted_iota(jnp.int32, (LANE, LANE), 0)
    columns = lax.broadcasted_iota(jnp.int32, (LANE, LANE), 1)
    gram = jnp.where((rows == columns) & (rows >= CHI), 1.0, total[:, 0:LANE])
    inverse = factor_inverse(gram, cholesky)
    products = [dot_exact(inverse, total[:, block(1 + n)]) for n in range(len(others))]
    high, low = split(inverse)
    both = jnp.concatenate([high, low], axis=0)
    for k in range(DD):
        joint = lax.dot_general(
            sketched[0:ROWS, block(k)], both, (((1,), (1,)), ((), ())),
            preferred_element_type=F32,
        )
        frame = joint[:, 0:LANE] + joint[:, LANE:]
        wide_frame[0:ROWS, block(k)] = frame.astype(BF)
        if k < MAIN:
            by_row[:, k, :] = frame[0:CHI]
        else:
            turned[:, CHI * MAIN : CHI * MAIN + ROWS] = frame.T[0:ROWS].astype(BF)
    flat = by_row[...].reshape(CHI * MAIN, LANE)
    turned[:, 0 : CHI * MAIN] = flat.T[0:ROWS].astype(BF)
    return products


def spread(edge_wide, by_row):
    for j in range(MAIN):
        by_row[:, j, :] = edge_wide[0:CHI, block(j)].astype(F32)


def absorb(by_row, edge_wide, near, arranged, rest, pushed):
    last = dot(edge_wide[0:ROWS, block(MAIN)], near[...])
    for k in range(DD):
        rest[:, k, :] = last[0:104, block(k)]

    def group(index, carry):
        first = index * GROUP
        left = by_row[pl.ds(first, GROUP)].reshape(GROUP * MAIN, LANE).astype(BF)
        mixed = dot(left, near[...])
        for batch in range(GROUP // BATCH):
            sides = []
            for side in range(BATCH):
                own = BATCH * batch + side
                sides.append(
                    jnp.concatenate(
                        [mixed[MAIN * own : MAIN * (own + 1), block(k)] for k in range(DD)]
                        + [rest[first + own], jnp.zeros((8, LANE), F32)],
                        axis=0,
                    ).astype(BF)
                )
            result = dot(arranged[...], jnp.concatenate(sides, axis=1))
            for pair in range(BATCH // 2):
                at = pl.multiple_of((first + BATCH * batch + 2 * pair) * MAIN, 16)
                for k in range(DD):
                    rows = slice(MAIN * k, MAIN * (k + 1))
                    pushed[k // 2, pl.ds(at, 2 * MAIN), block(k % 2)] = jnp.concatenate(
                        [result[rows, block(2 * pair)], result[rows, block(2 * pair + 1)]], axis=0
                    ).astype(BF)
            for side in range(BATCH):
                rest[first + BATCH * batch + side] = result[
                    MAIN * DD : MAIN * DD + 32, block(side)
                ]
        return carry

    lax.fori_loop(0, CHI // GROUP, group, 0)
    for k in range(DD):
        pushed[k // 2, CHI * MAIN : CHI * MAIN + ROWS, block(k % 2)] = jnp.concatenate(
            [rest[:, k, :], jnp.zeros((8, LANE), F32)], axis=0
        ).astype(BF)


def close(far, pushed, edge):
    def one(pair, total):
        value = dot(far[...], pushed[pair])
        edge[pair] = value
        return total + jnp.sum(value * value)

    total = lax.fori_loop(0, PAIRS, one, jnp.zeros((), F32))
    return jnp.sqrt(total / (CHI * DD * CHI) + 1e-06)


def narrow(edge, scale, dense, wide=None):
    for k in range(DD):
        value = (edge[k // 2, :, block(k % 2)] / scale).astype(BF)
        if wide is not None:
            wide[0:ROWS, block(k)] = value
        dense[:, CHI * k : CHI * (k + 1)] = value[0:CHI, 0:CHI]


def kernel(
    c1, c2, c4, t1, t2, t3, t4, tensors, pattern, s_below, s_above, s_right, s_left,
    o_left_top, o_left_edge, o_left_bottom, o_top_left, o_top_edge, o_top_right,
    c1_next, t1_next, far_left, far_top, corner_in,
    wide_a, wide_b, wide_c, wide_d, wide_e, wide_t, square_a, square_b,
    by_row, rest, pushed, edge, cholesky, turned, turned_top, dense, dense_top,
    corner_out, site_tensors, slices, packed, a_left, a_top, fetched, send, receive,
):
    col, row = lax.axis_index("col"), lax.axis_index("row")
    columns, rows = lax.axis_size("col"), lax.axis_size("row")
    right, left = lax.rem(col + 1, columns), lax.rem(col + columns - 1, columns)
    below, above = lax.rem(row + 1, rows), lax.rem(row + rows - 1, rows)
    to_above, to_below = (col, above), (col, below)
    to_right, to_diagonal = (right, row), (right, below)
    fetch = pltpu.make_async_copy(tensors, site_tensors, fetched)
    fetch.start()
    barrier = pltpu.get_barrier_semaphore()
    for device in (to_above, to_below, to_right, (left, row), to_diagonal, (left, above)):
        pl.semaphore_signal(barrier, inc=1, device_id=device, device_id_type=MESH)
    pl.semaphore_wait(barrier, 6)

    def ship(source, target, index, device):
        copy = pltpu.make_async_remote_copy(
            src_ref=source, dst_ref=target, send_sem=send.at[index],
            recv_sem=receive.at[index], device_id=device, device_id_type=MESH,
        )
        copy.start()
        return copy

    get_t1 = ship(t1, t1_next, 0, to_above)
    get_c1 = ship(c1, c1_next, 1, to_above)

    for ref in (wide_a, wide_b, wide_c, wide_d, wide_e):
        ref[...] = jnp.zeros_like(ref)
    rest[...] = jnp.zeros_like(rest)
    for pair in range(PAIRS):
        pushed[pair, CHI * MAIN + ROWS :, :] = jnp.zeros(
            (DEPTH - CHI * MAIN - ROWS, 2 * LANE), BF
        )
    pushed[PAIRS - 1, :, LANE:] = jnp.zeros((DEPTH, LANE), BF)
    for ref in (turned, turned_top):
        ref[:, CHI * MAIN + ROWS :] = jnp.zeros((ROWS, DEPTH - CHI * MAIN - ROWS), BF)
    widen(t2, wide_t)
    pad_square(c2, square_a)
    wide_d[0:ROWS, :] = dot(square_a[0:ROWS], wide_t[...]).astype(BF)
    widen(t3, wide_t)
    pad_square(c4, square_a)
    wide_b[0:ROWS, :] = dot(square_a[0:ROWS], wide_t[...]).astype(BF)

    def sketch_pair(sketch):
        pad_square_f32 = square_b
        pad_square_f32[...] = jnp.zeros_like(square_b)
        pad_square_f32[0:CHI, 0:CHI] = sketch[...]
        return jnp.concatenate(split(square_b[...]), axis=1)

    below_pair = sketch_pair(s_below)
    above_pair = sketch_pair(s_above)
    fetch.wait()
    arrange(site_tensors, pattern[0, 0], slices, packed, a_left, a_top)
    get_t1.wait()
    get_c1.wait()
    widen(t1_next, wide_t)
    pad_square(c1_next, square_a)
    wide_c[0:ROWS, :] = dot(square_a[0:ROWS], wide_t[...]).astype(BF)
    for k in range(DD):
        joint = dot(wide_b[0:ROWS, block(k)], below_pair) + dot(
            wide_c[0:ROWS, block(k)], above_pair
        )
        wide_a[0:ROWS, block(k)] = (joint[:, 0:LANE] + joint[:, LANE:]).astype(BF)
    bottom, top = frame_of(wide_a, (wide_b, wide_c), cholesky, wide_e, by_row, turned)
    corner_out[0] = rms(bottom)[0:CHI, 0:CHI].astype(BF)
    corner_out[1] = rms(top)[0:CHI, 0:CHI].astype(BF)
    get_far = ship(turned, far_left, 2, to_below)
    get_corner = ship(corner_out.at[1], corner_in, 3, to_below)
    put_bottom = ship(corner_out.at[0], o_left_bottom, 4, to_right)
    put_top = ship(corner_out.at[1], o_left_top, 5, to_diagonal)
    widen(t4, wide_t)
    spread(wide_t, by_row)
    absorb(by_row, wide_t, wide_e, a_left, rest, pushed)
    get_far.wait()
    scale = close(far_left, pushed, edge)
    narrow(edge, scale, dense, wide_c)
    put_edge = ship(dense, o_left_edge, 6, to_right)
    get_corner.wait()
    square_b[...] = jnp.zeros_like(square_b)
    square_b[0:CHI, 0:CHI] = corner_in[...].astype(F32)
    wide_b[0:ROWS, :] = dot(square_b[...].T[0:ROWS].astype(BF), wide_c[...]).astype(BF)
    right_pair = sketch_pair(s_right)
    left_pair = sketch_pair(s_left)
    for k in range(DD):
        joint = dot(wide_d[0:ROWS, block(k)], right_pair) + dot(
            wide_b[0:ROWS, block(k)], left_pair
        )
        wide_a[0:ROWS, block(k)] = (joint[:, 0:LANE] + joint[:, LANE:]).astype(BF)
    side, head = frame_of(wide_a, (wide_d, wide_b), cholesky, wide_e, by_row, turned_top)
    corner_out[2] = rms(side)[0:CHI, 0:CHI].astype(BF)
    corner_out[3] = rms(head).T[0:CHI, 0:CHI].astype(BF)
    get_far_top = ship(turned_top, far_top, 7, to_right)
    put_side = ship(corner_out.at[2], o_top_right, 8, to_below)
    put_head = ship(corner_out.at[3], o_top_left, 9, to_diagonal)
    widen(t1, wide_t)
    spread(wide_t, by_row)
    absorb(by_row, wide_t, wide_e, a_top, rest, pushed)
    get_far_top.wait()
    scale = close(far_top, pushed, edge)
    narrow(edge, scale, dense_top)
    put_top_edge = ship(dense_top, o_top_edge, 10, to_below)
    for copy in (put_bottom, put_top, put_edge, put_side, put_head, put_top_edge):
        copy.wait()


def arrange(tensors, index, slices, packed, a_left, a_top):
    count = tensors.shape[1]
    place = lax.broadcasted_iota(jnp.int32, (32, count * DD), 0) * count + index
    entry = lax.broadcasted_iota(jnp.int32, (32, count * DD), 1)
    pick = jnp.where(entry == place, 1.0, 0.0).astype(BF)
    for i in range(DD):
        several = tensors[DD * i : DD * (i + 1)].reshape(count * DD, DD * DD)
        rows = jnp.concatenate(
            [dot(pick, several), jnp.zeros((32, SQUARE - DD * DD), F32)], axis=1
        )
        slices[i] = rows.T
    margin = SQUARE - DD * DD

    def gather(kr, carry):
        pieces = [slices[0:MAIN, DD * kd + kr, 0:DD] for kd in range(DD)]
        packed[pl.ds(pl.multiple_of(kr * MAIN, 8), MAIN), :] = jnp.concatenate(
            pieces + [jnp.zeros((MAIN, margin), F32)], axis=1
        )
        return carry

    lax.fori_loop(0, DD, gather, 0)
    pieces = [slices[MAIN, DD * kd : DD * (kd + 1), 0:DD] for kd in range(DD)]
    last = jnp.concatenate(pieces + [jnp.zeros((DD, margin), F32)], axis=1)
    packed[DD * MAIN :, :] = jnp.concatenate(
        [last, jnp.zeros((SQUARE - DD * DD, SQUARE), F32)], axis=0
    )
    source = lax.broadcasted_iota(jnp.int32, (SQUARE, SQUARE), 0)
    target = lax.broadcasted_iota(jnp.int32, (1, SQUARE), 1)
    wanted = jnp.where(
        target < DD * MAIN,
        target + target // MAIN,
        jnp.where(target < DD * DD, (target - DD * MAIN) * DD + MAIN, -1),
    )
    choose = jnp.where(source == wanted, 1.0, 0.0).astype(BF)
    result = dot(packed[...].astype(BF), choose)
    a_left[...] = result.astype(BF)
    a_top[...] = result.T.astype(BF)


def hand_on(*refs):
    for source, target in zip(refs[:6], refs[6:]):
        target[...] = source[...]


def body(
    corner_top_left, corner_top_right, corner_bottom_left, edge_top, edge_right,
    edge_bottom, edge_left, tensors, pattern, sketch_below, sketch_above,
    sketch_right, sketch_left,
):
    corner = jax.ShapeDtypeStruct((CHI, CHI), BF)
    long = jax.ShapeDtypeStruct((CHI, DD * CHI), BF)
    vmem = pl.BlockSpec(memory_space=pltpu.VMEM)
    wide = pltpu.VMEM((LANE, WIDE), BF)
    by_leg = tensors.transpose(1, 0, 2)
    anywhere = pl.BlockSpec(memory_space=pl.ANY)
    shapes = (corner, long, corner, corner, long, corner)
    moved = pl.pallas_call(
        kernel,
        out_shape=shapes,
        in_specs=[vmem] * 7
        + [anywhere, pl.BlockSpec(memory_space=pltpu.SMEM)]
        + [vmem] * 4,
        out_specs=[anywhere] * 6,
        scratch_shapes=[
            pltpu.VMEM((CHI, CHI), BF),
            pltpu.VMEM((CHI, DD * CHI), BF),
            pltpu.VMEM((ROWS, DEPTH), BF),
            pltpu.VMEM((ROWS, DEPTH), BF),
            pltpu.VMEM((CHI, CHI), BF),
            wide, wide, wide, wide, wide, wide,
            pltpu.VMEM((LANE, LANE), BF),
            pltpu.VMEM((LANE, LANE), F32),
            pltpu.VMEM((CHI, MAIN, LANE), F32),
            pltpu.VMEM((104, 32, LANE), F32),
            pltpu.VMEM((PAIRS, DEPTH, 2 * LANE), BF),
            pltpu.VMEM((PAIRS, ROWS, 2 * LANE), F32),
            pltpu.VMEM((LANE, 2 * LANE), F32),
            pltpu.VMEM((ROWS, DEPTH), BF),
            pltpu.VMEM((ROWS, DEPTH), BF),
            pltpu.VMEM((CHI, DD * CHI), BF),
            pltpu.VMEM((CHI, DD * CHI), BF),
            pltpu.VMEM((4, CHI, CHI), BF),
            pltpu.VMEM(by_leg.shape, BF),
            pltpu.VMEM((DD, SQUARE, 32), F32),
            pltpu.VMEM((SQUARE, SQUARE), F32),
            pltpu.VMEM((SQUARE, SQUARE), BF),
            pltpu.VMEM((SQUARE, SQUARE), BF),
            pltpu.SemaphoreType.DMA(()),
            pltpu.SemaphoreType.DMA((11,)),
            pltpu.SemaphoreType.DMA((11,)),
        ],
        compiler_params=pltpu.CompilerParams(
            collective_id=0, has_side_effects=True, vmem_limit_bytes=60 * 1024 * 1024
        ),
    )(
        corner_top_left, corner_top_right, corner_bottom_left, edge_top, edge_right,
        edge_bottom, edge_left, by_leg, pattern, sketch_below, sketch_above,
        sketch_right, sketch_left,
    )
    return pl.pallas_call(
        hand_on,
        out_shape=shapes,
        in_specs=[vmem] * 6,
        out_specs=[vmem] * 6,
    )(*moved)


def solution(mesh):
    split_both = P("col", "row")
    in_specs = (split_both,) * 7 + (P(), split_both) + (P(),) * 4
    return jax.shard_map(
        body, mesh=mesh, in_specs=in_specs, out_specs=(split_both,) * 6, check_vma=False
    )
```

profile of v0, /device:TPU:0, one launch (start us, length us, event | category | flops | bytes accessed | tf_op | source)
XLA Modules:
  0.0 107.5 jit_solution(12030121481249852978)
XLA Ops:
  1.3 103.9 %shard_map.172 = (bf16[100,100]{1,0:T(8,128)(2,1)}, bf16[100,2500]{1,0:T(8,128)(2,1)}, bf16[100,100]{1,0:T(8,128)(2,1)}, bf16[100,100]{1,0:T(8,128)(2,1)}, bf16[...) custom-call(bf16[100,100]{1,0:T(8,128)(2,1)} %c1.1, bf16[100,100]{1,0:T(8,128)(2,1)} %c2.1, bf16[100,100]{1,0:T(8,128)(2,1)} %c4.1, ...), custom_call_target="tpu_custom_call" | custom-call | tf_op jit(solution)/shard_map/pallas_call | solution.py:368
  105.2 2.3 %shard_map.173 = (bf16[100,100]{1,0:T(8,128)(2,1)}, bf16[100,2500]{1,0:T(8,128)(2,1)}, bf16[100,100]{1,0:T(8,128)(2,1)}, bf16[100,100]{1,0:T(8,128)(2,1)}, bf16[...) custom-call(bf16[100,100]{1,0:T(8,128)(2,1)} %get-tuple-element.12.refs_0_, bf16[100,2500]{1,0:T(8,128)(2,1)} %get-tuple-element.13.refs_1_, ...), custom_call_target="tpu_custom_call" | custom-call | tf_op jit(solution)/shard_map/pallas_call | solution.py:411
where the time goes:
time: 108 us
  Pallas kernels  106 us (98%)
  between operations  1.29 us (1%)
    pallas_call x1, Pallas kernels, body(): pl.pallas_call(kernel, out_shape=shapes, in_specs=[vmem] * 7 + [anywhere,...  104 us
    pallas_call x1, Pallas kernels, body(): pl.pallas_call(hand_on, out_shape=shapes, in_specs=[vmem] * 6, out_specs=...  2.31 us

commit v1 on v0

--- a/solution.py
+++ b/solution.py
@@ -17,7 +17,9 @@
 DEPTH = 2560
 PAIRS = 13
 GROUP = 20
-BATCH = 2
+BATCH = 10
+LEAVING = (3, 7, 10, 12)
+RUNS = (0, 768, 1536, 2176, DEPTH)
 BF = jnp.bfloat16
 F32 = jnp.float32
 MESH = pl.DeviceIdType.MESH
@@ -150,27 +152,40 @@
         mixed = dot(left, near[...])
         for batch in range(GROUP // BATCH):
             sides = []
-            for side in range(BATCH):
-                own = BATCH * batch + side
-                sides.append(
-                    jnp.concatenate(
-                        [mixed[MAIN * own : MAIN * (own + 1), block(k)] for k in range(DD)]
-                        + [rest[first + own], jnp.zeros((8, LANE), F32)],
+            for side in range(2):
+                pieces = []
+                for entry in range(BATCH // 2):
+                    own = BATCH * batch + 2 * entry + side
+                    pieces.append(
+                        jnp.concatenate(
+                            [mixed[MAIN * own : MAIN * (own + 1), block(k)] for k in range(DD)]
+                            + [rest[first + own], jnp.zeros((8, LANE), F32)],
+                            axis=0,
+                        ).astype(BF)[:, 0:CHI]
+                    )
+                pieces.append(jnp.zeros((SQUARE, 4 * LANE - 5 * CHI), BF))
+                sides.append(jnp.concatenate(pieces, axis=1))
+            result = dot(arranged[...], jnp.concatenate(sides, axis=1))
+            for entry in range(BATCH // 2):
+                at = pl.multiple_of((first + BATCH * batch + 2 * entry) * MAIN, 16)
+                low = CHI * entry // LANE * LANE
+                high = -(-CHI * (entry + 1) // LANE) * LANE
+                offset = CHI * entry - low
+                margin = jnp.zeros((2 * MAIN, LANE - CHI), BF)
+                for k in range(DD):
+                    rows = slice(MAIN * k, MAIN * (k + 1))
+                    both = jnp.concatenate(
+                        [result[rows, low:high], result[rows, 4 * LANE + low : 4 * LANE + high]],
                         axis=0,
                     ).astype(BF)
-                )
-            result = dot(arranged[...], jnp.concatenate(sides, axis=1))
-            for pair in range(BATCH // 2):
-                at = pl.multiple_of((first + BATCH * batch + 2 * pair) * MAIN, 16)
-                for k in range(DD):
-                    rows = slice(MAIN * k, MAIN * (k + 1))
                     pushed[k // 2, pl.ds(at, 2 * MAIN), block(k % 2)] = jnp.concatenate(
-                        [result[rows, block(2 * pair)], result[rows, block(2 * pair + 1)]], axis=0
-                    ).astype(BF)
-            for side in range(BATCH):
-                rest[first + BATCH * batch + side] = result[
-                    MAIN * DD : MAIN * DD + 32, block(side)
-                ]
+                        [both[:, offset : offset + CHI], margin], axis=1
+                    )
+                for side in range(2):
+                    from_lane = 4 * LANE * side + CHI * entry
+                    rest[first + BATCH * batch + 2 * entry + side, :, 0:CHI] = result[
+                        MAIN * DD : MAIN * DD + 32, from_lane : from_lane + CHI
+                    ]
         return carry
 
     lax.fori_loop(0, CHI // GROUP, group, 0)
@@ -180,31 +195,53 @@
         ).astype(BF)
 
 
+def squares(values):
+    return jnp.sum((values * values).reshape(ROWS // 8, 8, 2 * LANE), axis=0)
+
+
+def inverse_scale(total):
+    return lax.rsqrt(jnp.sum(total) / (CHI * DD * CHI) + 1e-06)
+
+
 def close(far, pushed, edge):
-    def one(pair, total):
+    total = jnp.zeros((8, 2 * LANE), F32)
+    for pair in range(PAIRS):
         value = dot(far[...], pushed[pair])
         edge[pair] = value
-        return total + jnp.sum(value * value)
-
-    total = lax.fori_loop(0, PAIRS, one, jnp.zeros((), F32))
-    return jnp.sqrt(total / (CHI * DD * CHI) + 1e-06)
-
-
-def narrow(edge, scale, dense, wide=None):
-    for k in range(DD):
-        value = (edge[k // 2, :, block(k % 2)] / scale).astype(BF)
-        if wide is not None:
-            wide[0:ROWS, block(k)] = value
+        total = total + squares(value)
+    return inverse_scale(total)
+
+
+def close_out(far, pushed, dense, leave):
+    total = jnp.zeros((8, 2 * LANE), F32)
+    for pair in range(PAIRS):
+        value = dot(far[...], pushed[pair])
+        total = total + squares(value)
+        for side in range(2):
+            k = 2 * pair + side
+            if k < DD:
+                dense[:, CHI * k : CHI * (k + 1)] = value[
+                    :, LANE * side : LANE * side + CHI
+                ].astype(BF)
+        if pair in LEAVING:
+            leave(LEAVING.index(pair))
+    return inverse_scale(total)
+
+
+def narrow(edge, scale, dense, wide):
+    for k in range(DD):
+        value = (edge[k // 2, :, block(k % 2)] * scale).astype(BF)
+        wide[0:ROWS, block(k)] = value
         dense[:, CHI * k : CHI * (k + 1)] = value[0:CHI, 0:CHI]
 
 
 def kernel(
     c1, c2, c4, t1, t2, t3, t4, tensors, pattern, s_below, s_above, s_right, s_left,
-    o_left_top, o_left_edge, o_left_bottom, o_top_left, o_top_edge, o_top_right,
+    o_left_top, o_left_edge, o_left_bottom, o_top_left, o_top_edge, o_top_right, o_top_scale,
     c1_next, t1_next, far_left, far_top, corner_in,
     wide_a, wide_b, wide_c, wide_d, wide_e, wide_t, square_a, square_b,
     by_row, rest, pushed, edge, cholesky, turned, turned_top, dense, dense_top,
-    corner_out, site_tensors, slices, packed, a_left, a_top, fetched, send, receive,
+    corner_out, scale_out, site_tensors, slices, packed, a_left, a_top, fetched, send, receive,
 ):
     col, row = lax.axis_index("col"), lax.axis_index("row")
     columns, rows = lax.axis_size("col"), lax.axis_size("row")
@@ -238,6 +275,7 @@
             (DEPTH - CHI * MAIN - ROWS, 2 * LANE), BF
         )
     pushed[PAIRS - 1, :, LANE:] = jnp.zeros((DEPTH, LANE), BF)
+    dense_top[:, CHI * DD :] = jnp.zeros((ROWS, DEPTH - CHI * DD), BF)
     for ref in (turned, turned_top):
         ref[:, CHI * MAIN + ROWS :] = jnp.zeros((ROWS, DEPTH - CHI * MAIN - ROWS), BF)
     widen(t2, wide_t)
@@ -302,10 +340,19 @@
     spread(wide_t, by_row)
     absorb(by_row, wide_t, wide_e, a_top, rest, pushed)
     get_far_top.wait()
-    scale = close(far_top, pushed, edge)
-    narrow(edge, scale, dense_top)
-    put_top_edge = ship(dense_top, o_top_edge, 10, to_below)
-    for copy in (put_bottom, put_top, put_edge, put_side, put_head, put_top_edge):
+    leaving = []
+
+    def leave(run):
+        columns = pl.ds(RUNS[run], RUNS[run + 1] - RUNS[run])
+        leaving.append(
+            ship(dense_top.at[:, columns], o_top_edge.at[:, columns], 10 + run, to_below)
+        )
+
+    scale_out[...] = jnp.broadcast_to(
+        close_out(far_top, pushed, dense_top, leave), scale_out.shape
+    )
+    put_scale = ship(scale_out, o_top_scale, 14, to_below)
+    for copy in (put_bottom, put_top, put_edge, put_side, put_head, *leaving, put_scale):
         copy.wait()
 
 
@@ -314,23 +361,30 @@
     place = lax.broadcasted_iota(jnp.int32, (32, count * DD), 0) * count + index
     entry = lax.broadcasted_iota(jnp.int32, (32, count * DD), 1)
     pick = jnp.where(entry == place, 1.0, 0.0).astype(BF)
-    for i in range(DD):
+    blank = jnp.zeros((32, SQUARE), F32)
+
+    def of(i):
         several = tensors[DD * i : DD * (i + 1)].reshape(count * DD, DD * DD)
-        rows = jnp.concatenate(
+        return jnp.concatenate(
             [dot(pick, several), jnp.zeros((32, SQUARE - DD * DD), F32)], axis=1
         )
-        slices[i] = rows.T
+
+    for i in range(8):
+        after = of(MAIN) if i == 0 else blank
+        slices[i] = jnp.concatenate([of(i), of(i + 8), of(i + 16), after], axis=0).T
     margin = SQUARE - DD * DD
 
     def gather(kr, carry):
-        pieces = [slices[0:MAIN, DD * kd + kr, 0:DD] for kd in range(DD)]
-        packed[pl.ds(pl.multiple_of(kr * MAIN, 8), MAIN), :] = jnp.concatenate(
-            pieces + [jnp.zeros((MAIN, margin), F32)], axis=1
-        )
+        loaded = [slices[:, DD * kd + kr, :] for kd in range(DD)]
+        rows = []
+        for third in range(3):
+            pieces = [each[:, 32 * third : 32 * third + DD] for each in loaded]
+            rows.append(jnp.concatenate(pieces + [jnp.zeros((8, margin), F32)], axis=1))
+        packed[pl.ds(pl.multiple_of(kr * MAIN, 8), MAIN), :] = jnp.concatenate(rows, axis=0)
         return carry
 
     lax.fori_loop(0, DD, gather, 0)
-    pieces = [slices[MAIN, DD * kd : DD * (kd + 1), 0:DD] for kd in range(DD)]
+    pieces = [slices[0, DD * kd : DD * (kd + 1), 96 : 96 + DD] for kd in range(DD)]
     last = jnp.concatenate(pieces + [jnp.zeros((DD, margin), F32)], axis=1)
     packed[DD * MAIN :, :] = jnp.concatenate(
         [last, jnp.zeros((SQUARE - DD * DD, SQUARE), F32)], axis=0
@@ -349,8 +403,12 @@
 
 
 def hand_on(*refs):
-    for source, target in zip(refs[:6], refs[6:]):
-        target[...] = source[...]
+    scale = refs[6][0:1, 0:1]
+    for n, (source, target) in enumerate(zip(refs[:6], refs[7:])):
+        if n == 4:
+            target[...] = (source[0:CHI, 0 : CHI * DD].astype(F32) * scale).astype(BF)
+        else:
+            target[...] = source[...]
 
 
 def body(
@@ -364,14 +422,16 @@
     wide = pltpu.VMEM((LANE, WIDE), BF)
     by_leg = tensors.transpose(1, 0, 2)
     anywhere = pl.BlockSpec(memory_space=pl.ANY)
+    raw = jax.ShapeDtypeStruct((ROWS, DEPTH), BF)
+    scale = jax.ShapeDtypeStruct((8, LANE), F32)
     shapes = (corner, long, corner, corner, long, corner)
     moved = pl.pallas_call(
         kernel,
-        out_shape=shapes,
+        out_shape=(*shapes[:4], raw, corner, scale),
         in_specs=[vmem] * 7
         + [anywhere, pl.BlockSpec(memory_space=pltpu.SMEM)]
         + [vmem] * 4,
-        out_specs=[anywhere] * 6,
+        out_specs=[anywhere] * 7,
         scratch_shapes=[
             pltpu.VMEM((CHI, CHI), BF),
             pltpu.VMEM((CHI, DD * CHI), BF),
@@ -389,16 +449,17 @@
             pltpu.VMEM((ROWS, DEPTH), BF),
             pltpu.VMEM((ROWS, DEPTH), BF),
             pltpu.VMEM((CHI, DD * CHI), BF),
-            pltpu.VMEM((CHI, DD * CHI), BF),
+            pltpu.VMEM((ROWS, DEPTH), BF),
             pltpu.VMEM((4, CHI, CHI), BF),
+            pltpu.VMEM((8, LANE), F32),
             pltpu.VMEM(by_leg.shape, BF),
-            pltpu.VMEM((DD, SQUARE, 32), F32),
+            pltpu.VMEM((8, SQUARE, LANE), F32),
             pltpu.VMEM((SQUARE, SQUARE), F32),
             pltpu.VMEM((SQUARE, SQUARE), BF),
             pltpu.VMEM((SQUARE, SQUARE), BF),
             pltpu.SemaphoreType.DMA(()),
-            pltpu.SemaphoreType.DMA((11,)),
-            pltpu.SemaphoreType.DMA((11,)),
+            pltpu.SemaphoreType.DMA((15,)),
+            pltpu.SemaphoreType.DMA((15,)),
         ],
         compiler_params=pltpu.CompilerParams(
             collective_id=0, has_side_effects=True, vmem_limit_bytes=60 * 1024 * 1024
@@ -411,7 +472,7 @@
     return pl.pallas_call(
         hand_on,
         out_shape=shapes,
-        in_specs=[vmem] * 6,
+        in_specs=[vmem] * 7,
         out_specs=[vmem] * 6,
     )(*moved)
 

time: 108 us -> 99.2 us (0.919)
  Pallas kernels: 106 us -> 97.7 us
    pallas_call x2, Pallas kernels: 106 us -> 97.7 us  [the longest x1 95.4 us: body(): pl.pallas_call(kernel, out_shape=(*shapes[:4], raw, corner, scale), in_sp...]
where the time goes in v1:
time: 99.2 us; the launch traced here: 99 us
  Pallas kernels  97.7 us (98%)
  between operations  1.29 us (1%)
    pallas_call x1, Pallas kernels, body(): pl.pallas_call(kernel, out_shape=(*shapes[:4], raw, corner, scale), in_sp...  95.4 us
    pallas_call x1, Pallas kernels, body(): pl.pallas_call(hand_on, out_shape=shapes, in_specs=[vmem] * 7, out_specs=...  2.36 us

profile of v1, /device:TPU:0, one launch (start us, length us, event | category | flops | bytes accessed | tf_op | source)
XLA Modules:
  0.0 99.0 jit_solution(6834428359784286899)
XLA Ops:
  1.3 95.4 %shard_map.172 = (bf16[100,100]{1,0:T(8,128)(2,1)}, bf16[100,2500]{1,0:T(8,128)(2,1)}, bf16[100,100]{1,0:T(8,128)(2,1)}, bf16[100,100]{1,0:T(8,128)(2,1)}, bf16[...) custom-call(bf16[100,100]{1,0:T(8,128)(2,1)} %c1.1, bf16[100,100]{1,0:T(8,128)(2,1)} %c2.1, ...), custom_call_target="tpu_custom_call" | custom-call | tf_op jit(solution)/shard_map/pallas_call | solution.py:428
  96.7 2.4 %shard_map.173 = (bf16[100,100]{1,0:T(8,128)(2,1)}, bf16[100,2500]{1,0:T(8,128)(2,1)}, bf16[100,100]{1,0:T(8,128)(2,1)}, bf16[100,100]{1,0:T(8,128)(2,1)}, bf16[...) custom-call(bf16[100,100]{1,0:T(8,128)(2,1)} %get-tuple-element.13.refs_0_, bf16[100,2500]{1,0:T(8,128)(2,1)} %get-tuple-element.14.refs_1_, ...), custom_call_target="tpu_custom_call" | custom-call | tf_op jit(solution)/shard_map/pallas_call | solution.py:472
